TPU v7x, 32 devices: a whole 2x2x4 slice. The times are simulated.
32 devices in a mesh: groups: 2 (over y), leaf: 8 (over z, x), sub: 2 (over core).
Axes of the slice: x: 2, y: 2, z: 4, core: 2. Of those that a mesh axis runs over, the one named last changes fastest.
Arguments:
- points: float32 [131072, 32], P(('groups', 'leaf', 'sub')), parts along dimension 0
- rhs: float32 [131072, 16], P(('groups', 'leaf', 'sub')), parts along dimension 0, may hold values from -0.4 to 0.4
- leaf_interpolator: float32 [256, 128, 512], P(('groups', 'leaf', 'sub')), parts along dimension 0, may hold values from -0.25 to 0.25
- node_basis: float32 [32, 128, 1024], P(('groups', 'leaf', 'sub')), parts along dimension 0, may hold values from -0.1875 to 0.1875
- leaf_skeleton: int32 [256, 128], P(('groups', 'leaf', 'sub')), parts along dimension 0, may hold values from 0 to 511, as said below
- node_skeleton: int32 [32, 128], P(('groups', 'leaf', 'sub')), parts along dimension 0, may hold values from 0 to 1023, as said below
- near_list: int32 [256, 4], P(('groups', 'leaf', 'sub')), parts along dimension 0, may hold values from 0 to 127, as said below
- far_owner: int32 [256, 16, 1], P(('groups', 'leaf', 'sub')), parts along dimension 0, may hold values from 0 to 15; in each aligned block of 128 rows (0 to 127, 128 to 255, ..., all dimensions but the last counted through in order) at most 16 rows name the same one
- far_node: int32 [256, 16], P(('groups', 'leaf', 'sub')), parts along dimension 0, may hold values from 0 to 8
Outputs:
- product: float32 [131072, 16], P(('groups', 'leaf', 'sub')), parts along dimension 0
There are 2 independent parts, one for each index of `groups`. A program takes and returns all parts, laid end to end along the dimension named above; each array names one. Nothing has to cross between parts.
Inputs may be any that keep to these rules, and one draw needn't show every extreme that they name: `near_list`: entry 0 of each row is the row's own leaf; every entry lies within 8 leaves of it, and entry 1 lies exactly 8 leaves away. `leaf_skeleton`: the offsets of one row are distinct. `node_skeleton`: the positions of one row are distinct. `far_owner`: among the far entries of the leaves of one device, no owner is named more than 16 times, and in every draw some device names some owner exactly 16 times.
All inputs are finite; a program needn't handle non-finite values.
Results may differ from a plain program's by a relative error of at most 0.000076.
Values sent between devices are 32-bit elements; how exact they have to be, the bound alone decides.
A program may use at most 128 MiB of HBM per device.

v0:
```python
import functools
import math

import jax
import jax.numpy as jnp
from jax import lax
from jax.experimental import pallas as pl
from jax.experimental.pallas import tpu as pltpu
from jax.sharding import PartitionSpec as P

F32 = jnp.float32
BF16 = jnp.bfloat16
DEPTH = 256
NT = (((1,), (1,)), ((), ()))


def split2(x):
    hi = x.astype(BF16)
    return hi, (x - hi.astype(F32)).astype(BF16)


def split3(x):
    hi = x.astype(BF16)
    rest = x - hi.astype(F32)
    mid = rest.astype(BF16)
    return hi, mid, (rest - mid.astype(F32)).astype(BF16)


def norm_rows(norm, first):
    n1, n2, n3 = (part.astype(F32) for part in split3(norm))
    row = lax.broadcasted_iota(jnp.int32, (16, norm.shape[1]), 0)
    at = 0 if first else 3
    parts = jnp.where(row == at, n1, jnp.where(row == at + 1, n2, n3))
    inside = (row >= at) & (row < at + 3)
    return jnp.where(inside, parts, jnp.where(row < 6, 1.0, 0.0)).astype(BF16)


def features(x, norm, target):
    x1, x2, x3 = split3(x)
    order = (x1, x1, x2, x2, x1, x3) if target else (x1, x2, x1, x2, x3, x1)
    used = 6 * x.shape[0] + 16
    tail = jnp.zeros((DEPTH - used, x.shape[1]), BF16)
    return jnp.concatenate(order + (norm_rows(norm, target), tail), 0)


def target_features(x):
    scale = math.log2(math.e) / x.shape[0]
    norm = jnp.sum(x * x, 0, keepdims=True) * (-0.5 * scale)
    return features(x * scale, norm, True).T


def source_features(y):
    scale = math.log2(math.e) / y.shape[0]
    norm = jnp.sum(y * y, 0, keepdims=True) * (-0.5 * scale)
    return features(y, norm, False)


def tile(a, src, dims):
    b = source_features(src[:dims])
    w1, w2 = split2(src[dims:])
    weights = jnp.concatenate([w1, w2], 0)
    total = None
    for start in range(0, src.shape[1], 256):
        cut = slice(start, start + 256)
        k = jnp.exp2(jnp.dot(a, b[:, cut], preferred_element_type=F32))
        hi, lo = split2(k)
        w = weights[:, cut]
        part = lax.dot_general(
            jnp.concatenate([hi, lo], 1), jnp.concatenate([w, w], 1), NT,
            preferred_element_type=F32,
        )
        total = part if total is None else total + part
    return total


def prep_kernel(points, rhs, interp, basis, leaf_skel, node_skel, src, table):
    leaves, skel, size = interp.shape
    dims = points.shape[1]
    all_values, all_points = [], []
    for l in range(leaves):
        rows = slice(l * size, (l + 1) * size)
        xt = points[rows, :].T
        r = rhs[rows, :]
        src[l, :dims, :] = xt
        src[l, dims:, :] = r.T
        picks = lax.broadcasted_iota(jnp.int32, (size, skel), 0) == leaf_skel[l : l + 1, :]
        stacked = jnp.concatenate(split3(xt), 0)
        got = jnp.dot(stacked, picks.astype(BF16), preferred_element_type=F32)
        pts = got[:dims] + got[dims : 2 * dims] + got[2 * dims :]
        values = narrow_dot(interp[l], r)
        table[l, :dims, :] = pts
        table[l, dims:, :] = values.T
        all_values.append(values)
        all_points.append(pts)
    stack_points = jnp.concatenate(all_points, 1)
    picks = lax.broadcasted_iota(jnp.int32, (leaves * skel, skel), 0) == node_skel[0:1, :]
    stacked = jnp.concatenate(split3(stack_points), 0)
    got = jnp.dot(stacked, picks.astype(BF16), preferred_element_type=F32)
    table[leaves, :dims, :] = got[:dims] + got[dims : 2 * dims] + got[2 * dims :]
    values = narrow_dot(basis[0], jnp.concatenate(all_values, 0))
    table[leaves, dims:, :] = values.T


def narrow_dot(m, r):
    cols = r.shape[1]
    hi, lo = split2(m)
    parts = jnp.concatenate(split2(r), 1)
    got = jnp.dot(
        jnp.concatenate([hi, lo], 1), jnp.concatenate([parts, parts], 0),
        preferred_element_type=F32,
    )
    return got[:, :cols] + got[:, cols:]


def apply_kernel(ids, own, *refs, dims, per_tile, has_base):
    out = refs[-1]
    srcs = refs[: -2 if has_base else -1]
    a = target_features(own[0, :dims, :])
    total = None
    for t in range(0, len(srcs), per_tile):
        group = [ref[0] for ref in srcs[t : t + per_tile]]
        src = group[0] if per_tile == 1 else jnp.concatenate(group, 1)
        part = tile(a, src, dims)
        total = part if total is None else total + part
    cols = out.shape[1]
    result = total[:, :cols] + total[:, cols:]
    if has_base:
        result = result + refs[-2][...]
    out[...] = result


def run_apply(ids, own, table, base, columns, name):
    leaves, width, size = own.shape
    count = ids.shape[1]
    n = table.shape[2]
    pick = lambda f: lambda l, ids: (ids[l, f], 0, 0)
    in_specs = [pl.BlockSpec((1, width, size), lambda l, ids: (l, 0, 0))]
    in_specs += [pl.BlockSpec((1, width, n), pick(f)) for f in range(count)]
    operands = [own] + [table] * count
    if base is not None:
        in_specs.append(pl.BlockSpec((size, columns), lambda l, ids: (l, 0)))
        operands.append(base)
    entries = leaves * size * count * n
    return pl.pallas_call(
        functools.partial(
            apply_kernel, dims=width - columns, per_tile=max(1, size // n), has_base=base is not None
        ),
        grid_spec=pltpu.PrefetchScalarGridSpec(
            num_scalar_prefetch=1,
            grid=(leaves,),
            in_specs=in_specs,
            out_specs=pl.BlockSpec((size, columns), lambda l, ids: (l, 0)),
        ),
        out_shape=jax.ShapeDtypeStruct((leaves * size, columns), F32),
        compiler_params=pltpu.CompilerParams(vmem_limit_bytes=48 * 1024 * 1024),
        cost_estimate=pl.CostEstimate(
            flops=entries * 2 * 3 * 256, bytes_accessed=leaves * count * n * width * 4,
            transcendentals=entries,
        ),
        name=name,
    )(ids, *operands)


def shifted(value, axes):
    peers = lax.axis_size(axes)
    up = [(i, i + 1) for i in range(peers - 1)]
    down = [(j, i) for i, j in up]
    return lax.ppermute(value, axes, up), lax.ppermute(value, axes, down)


def per_device(
    points, rhs, leaf_interpolator, node_basis, leaf_skeleton, node_skeleton, near_list,
    far_owner, far_node,
):
    axes = ("leaf", "sub")
    leaves, skel, size = leaf_interpolator.shape
    dims, columns = points.shape[1], rhs.shape[1]
    width = dims + columns
    vmem = pl.BlockSpec(memory_space=pltpu.VMEM)
    src, table = pl.pallas_call(
        prep_kernel,
        in_specs=[vmem] * 6,
        out_specs=[vmem] * 2,
        out_shape=[
            jax.ShapeDtypeStruct((leaves, width, size), F32),
            jax.ShapeDtypeStruct((leaves + 1, width, skel), F32),
        ],
        compiler_params=pltpu.CompilerParams(vmem_limit_bytes=48 * 1024 * 1024),
        name="prep",
    )(points, rhs, leaf_interpolator, node_basis, leaf_skeleton, node_skeleton)
    every = lax.all_gather(table, axes, axis=0, tiled=True)
    before, after = shifted(src, axes)
    extended = jnp.concatenate([before, src, after], 0)
    near_ids = near_list - (lax.axis_index(axes) - 1) * leaves
    far_ids = far_owner[:, :, 0] * (leaves + 1) + far_node
    near = run_apply(near_ids, src, extended, None, columns, "near")
    return run_apply(far_ids, src, every, near, columns, "far")


def solution(mesh):
    rows = ("groups", "leaf", "sub")
    two, three = P(rows, None), P(rows, None, None)
    in_specs = (two, two, three, three, two, two, two, three, two)
    return jax.shard_map(
        per_device, mesh=mesh, in_specs=in_specs, out_specs=two, check_vma=False
    )
```

profile of v0, /device:TPU:13, one launch (start us, length us, event | category | flops | bytes accessed | tf_op | source)
XLA Modules:
  0.0 109.5 jit_solution(3287983083242738832)
XLA Ops:
  6.5 0.0 copy-start.7
  6.5 0.0 copy-start.3
  6.5 0.0 copy-start.5
  6.5 0.0 copy-start.6
  6.5 0.0 all-gather.2.cloned.1.call-start
  6.6 1.7 %copy.16.points = f32[4096,32]{1,0:T(8,128)S(1)} copy(f32[4096,32]{0,1:T(8,128)} %param.9) | data formatting | bytes 1048576 | tf_op args[0]
  8.3 0.0 copy-done.7
  8.3 1.9 %copy.17.rhs = f32[4096,16]{1,0:T(8,128)} copy(f32[4096,16]{0,1:T(8,128)S(1)} %copy-done.7) | data formatting | bytes 524288 | tf_op args[1]
  10.2 0.0 copy-done.3
  10.2 0.0 copy-done.5
  10.3 0.0 copy-done.6
  10.3 1.6 %copy-done = f32[4096,16]{1,0:T(8,128)S(1)} copy-done((f32[4096,16]{1,0:T(8,128)S(1)}, f32[4096,16]{1,0:T(8,128)}, u32[]{:S(2)}) %copy-start) | copy-done | bytes 262168
  11.8 0.0 copy-start.10
  11.9 5.7 %prep.1 = (f32[8,48,512]{2,1,0:T(8,128)S(1)}, f32[9,48,128]{2,1,0:T(8,128)S(1)}) custom-call(f32[4096,32]{1,0:T(8,128)S(1)} %copy.16.points, f32[4096,16]{1,0:T(8,128)S(1)} %copy-done, f32[8,128,512]{2,1,0:T(8,128)} %interp.1, f32[1,128,1024]{2,1,0:T(8,128)S(1)} %copy-done.3, s32[8,128]{1,0:T(8,128)S(1)} %copy-done.5, s32[1,128]{1,0:T(1,128)S(1)} %copy-done.6), custom_call_target="tpu_custom_call" | custom-call | tf_op jit(solution)/shard_map/prep/pallas_call | solution.py:180
  17.5 0.7 copy-done.4
  18.2 0.0 all-gather.2.cloned.1.call-update
  18.2 3.7 %collective-permute-start = (f32[8,48,512]{2,1,0:T(8,128)S(1)}, f32[8,48,512]{2,1,0:T(8,128)S(1)}, u32[]{:S(2)}, u32[]{:S(2)}) collective-permute-start(f32[8,48,512]{2,1,0:T(8,128)S(1)} %get-tuple-element.7.own), channel_id=1, source_target_pairs={{0,1},{1,2},{2,3},{3,4},{4,5},{5,6},{6,7},{7,8},{8,9},{9,10},{10,1... | collective-permute-start | bytes 2359304 | tf_op jit(solution)/shard_map/ppermute | solution.py:168
  21.9 1.9 %collective-permute-start.1 = (f32[8,48,512]{2,1,0:T(8,128)S(1)}, f32[8,48,512]{2,1,0:T(8,128)S(1)}, u32[]{:S(2)}, u32[]{:S(2)}) collective-permute-start(f32[8,48,512]{2,1,0:T(8,128)S(1)} %get-tuple-element.7.own), channel_id=1, source_target_pairs={{1,0},{2,1},{3,2},{4,3},{5,4},{6,5},{7,6},{8,7},{9,8},{10,9},{11,1... | collective-permute-start | bytes 2359304 | tf_op jit(solution)/shard_map/ppermute | solution.py:168
  23.9 0.0 copy-done.10
  23.9 0.1 copy.18
  24.0 0.0 copy-done.8
  24.0 0.0 copy-done.9
  24.0 17.6 %collective-permute-done = f32[8,48,512]{2,1,0:T(8,128)S(1)} collective-permute-done((f32[8,48,512]{2,1,0:T(8,128)S(1)}, f32[8,48,512]{2,1,0:T(8,128)S(1)}, u32[]{:S(2)}, u32[]{:S(2)}) %collective-permute-start) | collective-permute-done | bytes 786464 | tf_op jit(solution)/shard_map/ppermute | solution.py:168
  41.6 2.0 %collective-permute-done.1 = f32[8,48,512]{2,1,0:T(8,128)S(1)} collective-permute-done((f32[8,48,512]{2,1,0:T(8,128)S(1)}, f32[8,48,512]{2,1,0:T(8,128)S(1)}, u32[]{:S(2)}, u32[]{:S(2)}) %collective-permute-start.1) | collective-permute-done | bytes 786464 | tf_op jit(solution)/shard_map/ppermute | solution.py:168
  43.6 0.3 pad_maximum_fusion.refs_0_.refs_1_.refs_2_.refs_3_
  43.9 24.3 %near.1.refs_16_ = f32[4096,16]{1,0:T(8,128)S(1)} custom-call(s32[8,4]{1,0:T(8,128)S(1)} %broadcast_subtract_fusion.ids, f32[8,48,512]{2,1,0:T(8,128)S(1)} %get-tuple-element.7.own, f32[24,48,512]{2,1,0:T(8,128)S(1)} %pad_maximum_fusion.refs_0_.refs_1_.refs_2_.refs_3_, f32[24,48,512]{2,1,0:T(8,128)S(1)} %pad_maximum_fusion.refs_0_.refs_1_.refs_2_.refs_3_, ...), custom_call_target="tpu_custom_call" | custom-call | flops 12884901888 | bytes 3145728 | tf_op jit(solution)/shard_map/near/pallas_call | solution.py:144
  68.2 0.0 copy-start.1
  68.2 1.3 %copy-done.1 = f32[4096,16]{1,0:T(8,128)} copy-done((f32[4096,16]{1,0:T(8,128)}, f32[4096,16]{1,0:T(8,128)S(1)}, u32[]{:S(2)}) %copy-start.1) | copy-done | bytes 262168
  69.6 2.6 %all-gather.2.cloned.1.call-done.refs_0_.refs_1_.refs_2_.refs_3_.refs_4_.refs_5_.refs_6_.refs_7_.refs_8_.refs_9_.refs_10_.refs_11_.refs_12_.refs_13_.refs_14_.refs_15_ = f32[144,48,128]{2,1,0:T(8,128)} async-done(((f32[9,48,128]{2,1,0:T(8,128)}), f32[144,48,128]{2,1,0:T(8,128)}) %all-gather.2.cloned.1.call-update) | async-done | bytes 3538960 | tf_op jit(solution)/shard_map/all_gather | solution.py:191
  72.2 1.6 %copy-done.2 = f32[4096,16]{1,0:T(8,128)S(1)} copy-done((f32[4096,16]{1,0:T(8,128)S(1)}, f32[4096,16]{1,0:T(8,128)}, u32[]{:S(2)}) %copy-start.2) | copy-done | bytes 262168
  73.8 27.6 %far.1 = f32[4096,16]{1,0:T(8,128)S(1)} custom-call(s32[8,16]{1,0:T(8,128)S(1)} %bitcast_add_fusion.ids, f32[8,48,512]{2,1,0:T(8,128)S(1)} %get-tuple-element.7.own, f32[144,48,128]{2,1,0:T(8,128)} %all-gather.2.cloned.1.call-done.refs_0_.refs_1_.refs_2_.refs_3_.refs_4_.refs_5_.refs_6_.refs_7_.refs_8_.refs_9_.refs_10_.refs_11_.refs_12_.refs_13_.refs_14_.refs_15_, ...), custom_call_target="tpu_custom_call" | custom-call | flops 12884901888 | bytes 3145728 | tf_op jit(solution)/shard_map/far/pallas_call | solution.py:144
  101.4 1.3 %copy.19 = f32[4096,16]{0,1:T(8,128)} copy(f32[4096,16]{1,0:T(8,128)S(1)} %far.1) | data formatting | bytes 524288 | tf_op jit(solution)/shard_map/far/pallas_call | solution.py:144
  (7 shorter events, 0.0 us)
Async XLA Ops:
  6.5 1.8 %copy-start.7 = (f32[4096,16]{0,1:T(8,128)S(1)}, f32[4096,16]{0,1:T(8,128)}, u32[]{:S(2)}) copy-start(f32[4096,16]{0,1:T(8,128)} %param.10) | copy-start | bytes 786436
  6.5 3.7 %copy-start.3 = (f32[1,128,1024]{2,1,0:T(8,128)S(1)}, f32[1,128,1024]{2,1,0:T(8,128)}, u32[]{:S(2)}) copy-start(f32[1,128,1024]{2,1,0:T(8,128)} %basis.1) | copy-start | bytes 1572868
  6.5 3.7 %copy-start.5 = (s32[8,128]{1,0:T(8,128)S(1)}, s32[8,128]{1,0:T(8,128)}, u32[]{:S(2)}) copy-start(s32[8,128]{1,0:T(8,128)} %leaf_skel.1) | copy-start | bytes 12292
  6.5 3.7 %copy-start.6 = (s32[1,128]{1,0:T(1,128)S(1)}, s32[1,128]{1,0:T(1,128)}, u32[]{:S(2)}) copy-start(s32[1,128]{1,0:T(1,128)} %node_skel.1) | copy-start | bytes 1540
  6.5 65.7 %all-gather.2.cloned.1.call-start = ((), (), s32[]{:S(2)}) async-start(), calls=%async_computation | async-start | bytes 3760128 | tf_op jit(solution)/shard_map/all_gather | solution.py:191
  10.3 1.6 %copy-start = (f32[4096,16]{1,0:T(8,128)S(1)}, f32[4096,16]{1,0:T(8,128)}, u32[]{:S(2)}) copy-start(f32[4096,16]{1,0:T(8,128)} %copy.17.rhs) | copy-start | bytes 786436
  11.8 12.0 %copy-start.10 = (s32[8,4]{0,1:T(4,128)S(1)}, s32[8,4]{0,1:T(4,128)}, u32[]{:S(2)}) copy-start(s32[8,4]{0,1:T(4,128)} %param.15) | copy-start | bytes 388
  11.8 12.1 %copy-start.8 = (s32[8,16]{1,0:T(8,128)S(1)}, s32[8,16]{1,0:T(8,128)}, u32[]{:S(2)}) copy-start(s32[8,16]{1,0:T(8,128)} %param.17) | copy-start | bytes 1540
  11.9 12.1 %copy-start.9 = (s32[8,16,1]{1,2,0:T(1,128)S(1)}, s32[8,16,1]{1,2,0:T(1,128)}, u32[]{:S(2)}) copy-start(s32[8,16,1]{1,2,0:T(1,128)} %param.16) | copy-start | bytes 1540
  17.5 0.7 copy-start.4
  18.2 23.3 %collective-permute-start = (f32[8,48,512]{2,1,0:T(8,128)S(1)}, f32[8,48,512]{2,1,0:T(8,128)S(1)}, u32[]{:S(2)}, u32[]{:S(2)}) collective-permute-start(f32[8,48,512]{2,1,0:T(8,128)S(1)} %get-tuple-element.7.own), channel_id=1, source_target_pairs={{0,1},{1,2},{2,3},{3,4},{4,5},{5,6},{6,7},{7,8},{8,9},{9,10},{10,1... | collective-permute-start | bytes 2359304 | tf_op jit(solution)/shard_map/ppermute | solution.py:168
  21.9 21.7 %collective-permute-start.1 = (f32[8,48,512]{2,1,0:T(8,128)S(1)}, f32[8,48,512]{2,1,0:T(8,128)S(1)}, u32[]{:S(2)}, u32[]{:S(2)}) collective-permute-start(f32[8,48,512]{2,1,0:T(8,128)S(1)} %get-tuple-element.7.own), channel_id=1, source_target_pairs={{1,0},{2,1},{3,2},{4,3},{5,4},{6,5},{7,6},{8,7},{9,8},{10,9},{11,1... | collective-permute-start | bytes 2359304 | tf_op jit(solution)/shard_map/ppermute | solution.py:168
  68.2 1.3 %copy-start.1 = (f32[4096,16]{1,0:T(8,128)}, f32[4096,16]{1,0:T(8,128)S(1)}, u32[]{:S(2)}) copy-start(f32[4096,16]{1,0:T(8,128)S(1)} %near.1.refs_16_) | copy-start | bytes 786436
  72.2 1.6 %copy-start.2 = (f32[4096,16]{1,0:T(8,128)S(1)}, f32[4096,16]{1,0:T(8,128)}, u32[]{:S(2)}) copy-start(f32[4096,16]{1,0:T(8,128)} %copy-done.1) | copy-start | bytes 786436
Sparse Core Ops, SparseCore 0:
  18.4 53.7 all-gather.1
where the time goes:
time: 110 us
  Pallas kernels  57.6 us (52%)
  waiting for transfers between devices  22.3 us (20%)
  between operations  13.5 us (12%)
  local copies, waits for them, and re-layouts  10.2 us (9%)
  starting transfers between devices  5.63 us (5%)
    pallas_call x2, Pallas kernels, run_apply(): pl.pallas_call(functools.partial(apply_kernel, dims=width - columns, per_...  51.9 us
    ppermute x2, waiting for transfers between devices, shifted(): return (lax.ppermute(value, axes, up), lax.ppermute(value, axes, down))  19.7 us
    unnamed x25, local copies, waits for them, and re-layouts  8.95 us
    pallas_call x1, Pallas kernels, per_device(): pl.pallas_call(prep_kernel, in_specs=[vmem] * 6, out_specs=[vmem] * 2, ou...  5.66 us
    ppermute x2, starting transfers between devices, shifted(): return (lax.ppermute(value, axes, up), lax.ppermute(value, axes, down))  5.6 us
    all_gather x1, waiting for transfers between devices, per_device(): every = lax.all_gather(table, axes, axis=0, tiled=True)  2.64 us
  transfers between devices with their start and end apart: 3, of which 3 were waited for; matrix products, arithmetic and copies ran while one was open for 0% of the time, Pallas kernels for 22%

commit v1 on v0

v1 whole, which is shorter than its diff:
```python
import functools
import math

import jax
import jax.numpy as jnp
from jax import lax
from jax.experimental import pallas as pl
from jax.experimental.pallas import tpu as pltpu
from jax.sharding import PartitionSpec as P

F32 = jnp.float32
BF16 = jnp.bfloat16
DEPTH = 256
NT = (((1,), (1,)), ((), ()))


def split2(x):
    hi = x.astype(BF16)
    return hi, (x - hi.astype(F32)).astype(BF16)


def split3(x):
    hi = x.astype(BF16)
    rest = x - hi.astype(F32)
    mid = rest.astype(BF16)
    return hi, mid, (rest - mid.astype(F32)).astype(BF16)


def norm_rows(norm, first):
    n1, n2, n3 = (part.astype(F32) for part in split3(norm))
    row = lax.broadcasted_iota(jnp.int32, (16, norm.shape[1]), 0)
    at = 0 if first else 3
    parts = jnp.where(row == at, n1, jnp.where(row == at + 1, n2, n3))
    inside = (row >= at) & (row < at + 3)
    return jnp.where(inside, parts, jnp.where(row < 6, 1.0, 0.0)).astype(BF16)


def features(x, norm, target):
    x1, x2, x3 = split3(x)
    order = (x1, x1, x2, x2, x1, x3) if target else (x1, x2, x1, x2, x3, x1)
    used = 6 * x.shape[0] + 16
    tail = jnp.zeros((DEPTH - used, x.shape[1]), BF16)
    return jnp.concatenate(order + (norm_rows(norm, target), tail), 0)


def target_features(x):
    scale = math.log2(math.e) / x.shape[0]
    norm = jnp.sum(x * x, 0, keepdims=True) * (-0.5 * scale)
    return features(x * scale, norm, True).T


def source_features(y):
    scale = math.log2(math.e) / y.shape[0]
    norm = jnp.sum(y * y, 0, keepdims=True) * (-0.5 * scale)
    return features(y, norm, False)


def tile(a, src, dims):
    b = source_features(src[:dims])
    w1, w2 = split2(src[dims:])
    weights = jnp.concatenate([w1, w2], 0)
    total = None
    for start in range(0, src.shape[1], 256):
        cut = slice(start, start + 256)
        k = jnp.exp2(jnp.dot(a, b[:, cut], preferred_element_type=F32))
        hi, lo = split2(k)
        w = weights[:, cut]
        part = lax.dot_general(
            jnp.concatenate([hi, lo], 1), jnp.concatenate([w, w], 1), NT,
            preferred_element_type=F32,
        )
        total = part if total is None else total + part
    return total


def values_t(rt, m):
    cols = rt.shape[0]
    parts = jnp.concatenate(split2(rt), 0)
    hi, lo = split2(m)
    got = lax.dot_general(
        jnp.concatenate([parts, parts], 1), jnp.concatenate([hi, lo], 1), NT,
        preferred_element_type=F32,
    )
    return got[:cols] + got[cols:]


def picked_columns(xt, row):
    dims, size = xt.shape
    picks = lax.broadcasted_iota(jnp.int32, (size, row.shape[1]), 0) == row
    stacked = jnp.concatenate(split3(xt), 0)
    got = jnp.dot(stacked, picks.astype(BF16), preferred_element_type=F32)
    return got[:dims] + got[dims : 2 * dims] + got[2 * dims :]


def whole_kernel(
    points, rhs, interp, basis, leaf_skel, node_skel, near_list, far_owner, far_node,
    out, near, table, a_all, acc, near_send, near_recv, right_send, left_send, pair_send, recv,
):
    leaves, skel, size = interp.shape
    dims, columns = points.shape[0], rhs.shape[0]
    ring = lax.axis_size("leaf")
    leaf, sub = lax.axis_index("leaf"), lax.axis_index("sub")
    flat = leaf * 2 + sub
    devices = ring * 2
    half = ring // 2
    other = ring - 1 - half

    def leaf_at(position):
        q = lax.rem(position + ring, ring)
        return jnp.where(q < half, 2 * q, 2 * (ring - 1 - q) + 1)

    here = jnp.where(leaf % 2 == 0, leaf // 2, ring - 1 - leaf // 2)
    right = {"leaf": leaf_at(here + 1), "sub": sub}
    left = {"leaf": leaf_at(here - 1), "sub": sub}
    pair = {"leaf": leaf, "sub": 1 - sub}
    up_flat, down_flat = lax.rem(flat + 1, devices), lax.rem(flat + devices - 1, devices)
    up = {"leaf": up_flat // 2, "sub": up_flat % 2}
    down = {"leaf": down_flat // 2, "sub": down_flat % 2}

    barrier = pltpu.get_barrier_semaphore()
    for peer in (right, left, pair, up, down):
        pl.semaphore_signal(barrier, inc=1, device_id=peer, device_id_type=pl.DeviceIdType.MESH)
    for l in range(leaves):
        cut = slice(l * size, (l + 1) * size)
        near[leaves + l, :dims, :] = points[:, cut]
        near[leaves + l, dims:, :] = rhs[:, cut]

    @pl.when(flat == 0)
    def _():
        near[0:leaves] = jnp.zeros((leaves,) + near.shape[1:], F32)

    @pl.when(flat == devices - 1)
    def _():
        near[2 * leaves : 3 * leaves] = jnp.zeros((leaves,) + near.shape[1:], F32)

    pl.semaphore_wait(barrier, 5)

    def near_copy(to, first, which):
        return pltpu.make_async_remote_copy(
            src_ref=near.at[pl.ds(leaves, leaves)], dst_ref=near.at[pl.ds(first, leaves)],
            send_sem=near_send.at[which], recv_sem=near_recv.at[which],
            device_id=to, device_id_type=pl.DeviceIdType.MESH,
        )

    to_up, to_down = near_copy(up, 0, 0), near_copy(down, 2 * leaves, 1)

    @pl.when(flat < devices - 1)
    def _():
        to_up.start()

    @pl.when(flat > 0)
    def _():
        to_down.start()

    def block_copy(position, core, to, send):
        slot = leaf_at(position) * 2 + core
        return pltpu.make_async_remote_copy(
            src_ref=table.at[slot], dst_ref=table.at[slot],
            send_sem=send, recv_sem=recv.at[slot],
            device_id=to, device_id_type=pl.DeviceIdType.MESH,
        )

    def to_right(s):
        return block_copy(here - s, sub, right, right_send.at[s])

    def to_left(s):
        return block_copy(here + s, sub, left, left_send.at[s])

    def to_pair(position):
        q = lax.rem(position + ring, ring)
        return block_copy(position, sub, pair, pair_send.at[q])

    all_values, all_points = [], []
    for l in range(leaves):
        cut = slice(l * size, (l + 1) * size)
        pts = picked_columns(points[:, cut], leaf_skel[l : l + 1, :])
        values = values_t(rhs[:, cut], interp[l])
        table[flat, l, :dims, :] = pts
        table[flat, l, dims:, :] = values
        all_values.append(values)
        all_points.append(pts)
    table[flat, leaves, :dims, :] = picked_columns(jnp.concatenate(all_points, 1), node_skel[0:1, :])
    table[flat, leaves, dims:, :] = values_t(jnp.concatenate(all_values, 1), basis[0])
    to_right(0).start()
    to_left(0).start()
    to_pair(here).start()

    def own_tile(l, carry):
        block = near[leaves + l]
        a_all[l] = target_features(block[:dims])
        acc[l] = tile(a_all[l], block, dims)
        return carry

    lax.fori_loop(0, leaves, own_tile, 0)

    @pl.when(flat < devices - 1)
    def _():
        to_up.wait_send()
        to_down.wait_recv()

    @pl.when(flat > 0)
    def _():
        to_down.wait_send()
        to_up.wait_recv()

    def ring_step(s, carry):
        block_copy(here - 1 - s, sub, right, right_send.at[s]).wait_recv()

        @pl.when(s + 1 < half)
        def _():
            to_right(s + 1).start()

        to_pair(here - 1 - s).start()

        @pl.when(s < other)
        def _():
            block_copy(here + 1 + s, sub, left, left_send.at[s]).wait_recv()

            @pl.when(s + 1 < other)
            def _():
                to_left(s + 1).start()

            to_pair(here + 1 + s).start()

        return carry

    def near_tiles(l, carry):
        a = a_all[l]
        total = acc[l]
        for n in range(1, near_list.shape[1]):
            place = near_list[l, n] - (flat - 1) * leaves
            block = near[jnp.clip(place, 0, 3 * leaves - 1)]
            total = total + tile(a, block, dims)
        acc[l] = total
        return lax.fori_loop(l * half // leaves, (l + 1) * half // leaves, ring_step, carry)

    lax.fori_loop(0, leaves, near_tiles, 0)

    def finish(q, carry):
        block_copy(q, 1 - sub, pair, pair_send.at[q]).wait_recv()
        block_copy(q, sub, pair, pair_send.at[q]).wait_send()
        return carry

    lax.fori_loop(0, ring, finish, 0)
    for s in range(half):
        to_right(s).wait_send()
    for s in range(other):
        to_left(s).wait_send()

    def far_tiles(l, carry):
        a = a_all[l]
        total = acc[l]
        per_tile = size // skel
        for f in range(0, far_node.shape[1], per_tile):
            group = [table[far_owner[l, i], far_node[l, i]] for i in range(f, f + per_tile)]
            total = total + tile(a, jnp.concatenate(group, 1), dims)
        out[l] = (total[:, :columns] + total[:, columns:]).T
        return carry

    lax.fori_loop(0, leaves, far_tiles, 0)


def per_device(
    points, rhs, leaf_interpolator, node_basis, leaf_skeleton, node_skeleton, near_list,
    far_owner, far_node,
):
    leaves, skel, size = leaf_interpolator.shape
    dims, columns = points.shape[1], rhs.shape[1]
    width = dims + columns
    ring = lax.axis_size("leaf")
    vmem = pl.BlockSpec(memory_space=pltpu.VMEM)
    smem = pl.BlockSpec(memory_space=pltpu.SMEM)
    entries = leaves * size * size * 8
    dma = pltpu.SemaphoreType.DMA
    out = pl.pallas_call(
        whole_kernel,
        in_specs=[vmem] * 6 + [smem] * 3,
        out_specs=vmem,
        out_shape=jax.ShapeDtypeStruct((leaves, columns, size), F32),
        scratch_shapes=[
            pltpu.VMEM((3 * leaves, width, size), F32),
            pltpu.VMEM((2 * ring, leaves + 1, width, skel), F32),
            pltpu.VMEM((leaves, size, DEPTH), BF16),
            pltpu.VMEM((leaves, size, 2 * columns), F32),
            dma((2,)), dma((2,)), dma((ring,)), dma((ring,)), dma((ring,)), dma((2 * ring,)),
        ],
        compiler_params=pltpu.CompilerParams(
            vmem_limit_bytes=56 * 1024 * 1024, collective_id=0, has_side_effects=True
        ),
        cost_estimate=pl.CostEstimate(
            flops=entries * 2 * 3 * 256, bytes_accessed=8 * 1024 * 1024, transcendentals=entries
        ),
        name="whole",
    )(
        points.T, rhs.T, leaf_interpolator, node_basis, leaf_skeleton, node_skeleton, near_list,
        far_owner[:, :, 0], far_node,
    )
    return out.transpose(0, 2, 1).reshape(leaves * size, columns)


def solution(mesh):
    rows = ("groups", "leaf", "sub")
    two, three = P(rows, None), P(rows, None, None)
    in_specs = (two, two, three, three, two, two, two, three, two)
    return jax.shard_map(
        per_device, mesh=mesh, in_specs=in_specs, out_specs=two, check_vma=False
    )
```

time: 110 us -> 79 us (0.72)
  waiting for transfers between devices: 22.3 us -> 0 us
  Pallas kernels: 57.6 us -> 75.1 us
  between operations: 13.5 us -> 0.01 us
  local copies, waits for them, and re-layouts: 10.2 us -> 3.02 us
  starting transfers between devices: 5.63 us -> 0 us
    ppermute x2 -> x0, waiting for transfers between devices: 19.7 us -> none  [shifted(): return (lax.ppermute(value, axes, up), lax.ppermute(value, axes, down))]
    pallas_call x3 -> x1, Pallas kernels: 57.6 us -> 75.1 us  [per_device(): pl.pallas_call(whole_kernel, in_specs=[vmem] * 6 + [smem] * 3, out_specs=...]
    unnamed x25 -> x1, local copies, waits for them, and re-layouts: 8.95 us -> 1.35 us
    ppermute x2 -> x0, starting transfers between devices: 5.6 us -> none  [shifted(): return (lax.ppermute(value, axes, up), lax.ppermute(value, axes, down))]
    all_gather x1 -> x0, waiting for transfers between devices: 2.64 us -> none  [per_device(): every = lax.all_gather(table, axes, axis=0, tiled=True)]
    reshape x0 -> x1, local copies, waits for them, and re-layouts: none -> 1.67 us  [per_device(): return out.transpose(0, 2, 1).reshape(leaves * size, columns)]
    pallas_call x1 -> x0, local copies, waits for them, and re-layouts: 1.28 us -> none  [run_apply(): pl.pallas_call(functools.partial(apply_kernel, dims=width - columns, per_...]
  transfers between devices with their start and end apart: 3 -> 0, of which waited for: 3 -> 0; matrix products, arithmetic and copies ran while one was open for 0% -> 0% of each run, Pallas kernels for 22% -> 0%
where the time goes in v1:
time: 79 us; the launch traced here: 78.1 us
  Pallas kernels  75.1 us (95%)
  local copies, waits for them, and re-layouts  3.02 us (4%)
    pallas_call x1, Pallas kernels, per_device(): pl.pallas_call(whole_kernel, in_specs=[vmem] * 6 + [smem] * 3, out_specs=...  75.1 us
    reshape x1, local copies, waits for them, and re-layouts, per_device(): return out.transpose(0, 2, 1).reshape(leaves * size, columns)  1.67 us

profile of v1, /device:TPU:13, one launch (start us, length us, event | category | flops | bytes accessed | tf_op | source)
XLA Modules:
  0.0 78.1 jit_solution(15291427212274919721)
XLA Ops:
  0.0 1.3 %copy.11.near_list = s32[8,4]{1,0:T(8,128)} copy(s32[8,4]{0,1:T(4,128)} %param.15) | data formatting | bytes 256 | tf_op args[6]
  1.3 75.1 %whole.1 = f32[8,16,512]{2,1,0:T(8,128)} custom-call(f32[32,4096]{1,0:T(8,128)} %bitcast.7, f32[16,4096]{1,0:T(8,128)} %bitcast.8, f32[8,128,512]{2,1,0:T(8,128)} %interp.1, f32[1,128,1024]{2,1,0:T(8,128)} %basis.1, s32[8,128]{1,0:T(8,128)} %leaf_skel.1, s32[1,128]{1,0:T(1,128)} %node_skel.1, s32[8,4]{1,0:T(8,128)} %copy.11.near_list, s32[8,16]{1,0:T(8,128)} %bitcast.9, ...), custom_call_target="tpu_custom_call" | custom-call | flops 25769803776 | bytes 8388608 | tf_op jit(solution)/shard_map/whole/pallas_call | solution.py:275
  76.5 1.7 %copy.13 = f32[8,2,8,512]{3,2,0,1:T(8,128)} copy(f32[8,2,8,512]{3,2,1,0:T(8,128)} %bitcast.6) | data formatting | bytes 524288 | tf_op jit(solution)/shard_map/reshape | solution.py:298

commit v2 on v1

--- a/solution.py
+++ b/solution.py
@@ -46,7 +46,7 @@
 def target_features(x):
     scale = math.log2(math.e) / x.shape[0]
     norm = jnp.sum(x * x, 0, keepdims=True) * (-0.5 * scale)
-    return features(x * scale, norm, True).T
+    return features(x * scale, norm, True)
 
 
 def source_features(y):
@@ -56,21 +56,13 @@
 
 
 def tile(a, src, dims):
-    b = source_features(src[:dims])
-    w1, w2 = split2(src[dims:])
-    weights = jnp.concatenate([w1, w2], 0)
-    total = None
-    for start in range(0, src.shape[1], 256):
-        cut = slice(start, start + 256)
-        k = jnp.exp2(jnp.dot(a, b[:, cut], preferred_element_type=F32))
-        hi, lo = split2(k)
-        w = weights[:, cut]
-        part = lax.dot_general(
-            jnp.concatenate([hi, lo], 1), jnp.concatenate([w, w], 1), NT,
-            preferred_element_type=F32,
-        )
-        total = part if total is None else total + part
-    return total
+    b = source_features(src[:dims]).T
+    weights = jnp.concatenate(split2(src[dims:]), 0)
+    k = jnp.exp2(jnp.dot(b, a, preferred_element_type=F32))
+    return jnp.dot(
+        jnp.concatenate([weights, weights], 1), jnp.concatenate(split2(k), 0),
+        preferred_element_type=F32,
+    )
 
 
 def values_t(rt, m):
@@ -227,8 +219,8 @@
     def near_tiles(l, carry):
         a = a_all[l]
         total = acc[l]
-        for n in range(1, near_list.shape[1]):
-            place = near_list[l, n] - (flat - 1) * leaves
+        for n in range(1, near_list.shape[0]):
+            place = near_list[n, l] - (flat - 1) * leaves
             block = near[jnp.clip(place, 0, 3 * leaves - 1)]
             total = total + tile(a, block, dims)
         acc[l] = total
@@ -254,7 +246,8 @@
         for f in range(0, far_node.shape[1], per_tile):
             group = [table[far_owner[l, i], far_node[l, i]] for i in range(f, f + per_tile)]
             total = total + tile(a, jnp.concatenate(group, 1), dims)
-        out[l] = (total[:, :columns] + total[:, columns:]).T
+        cut = pl.ds(pl.multiple_of(l * size, size), size)
+        out[:, cut] = total[:columns] + total[columns:]
         return carry
 
     lax.fori_loop(0, leaves, far_tiles, 0)
@@ -276,12 +269,12 @@
         whole_kernel,
         in_specs=[vmem] * 6 + [smem] * 3,
         out_specs=vmem,
-        out_shape=jax.ShapeDtypeStruct((leaves, columns, size), F32),
+        out_shape=jax.ShapeDtypeStruct((columns, leaves * size), F32),
         scratch_shapes=[
             pltpu.VMEM((3 * leaves, width, size), F32),
             pltpu.VMEM((2 * ring, leaves + 1, width, skel), F32),
-            pltpu.VMEM((leaves, size, DEPTH), BF16),
-            pltpu.VMEM((leaves, size, 2 * columns), F32),
+            pltpu.VMEM((leaves, DEPTH, size), BF16),
+            pltpu.VMEM((leaves, 2 * columns, size), F32),
             dma((2,)), dma((2,)), dma((ring,)), dma((ring,)), dma((ring,)), dma((2 * ring,)),
         ],
         compiler_params=pltpu.CompilerParams(
@@ -292,10 +285,10 @@
         ),
         name="whole",
     )(
-        points.T, rhs.T, leaf_interpolator, node_basis, leaf_skeleton, node_skeleton, near_list,
+        points.T, rhs.T, leaf_interpolator, node_basis, leaf_skeleton, node_skeleton, near_list.T,
         far_owner[:, :, 0], far_node,
     )
-    return out.transpose(0, 2, 1).reshape(leaves * size, columns)
+    return out.T
 
 
 def solution(mesh):

time: 79 us -> 66.7 us (0.84)
  Pallas kernels: 75.1 us -> 64.9 us
  local copies, waits for them, and re-layouts: 3.02 us -> 1.67 us
    pallas_call x1, Pallas kernels: 75.1 us -> 64.9 us  [per_device(): pl.pallas_call(whole_kernel, in_specs=[vmem] * 6 + [smem] * 3, out_specs=...]
    reshape x1 -> x0, local copies, waits for them, and re-layouts: 1.67 us -> none  [per_device(): return out.transpose(0, 2, 1).reshape(leaves * size, columns)]
where the time goes in v2:
time: 66.7 us; the launch traced here: 66.6 us
  Pallas kernels  64.9 us (97%)
  local copies, waits for them, and re-layouts  1.67 us (3%)
    pallas_call x1, Pallas kernels, per_device(): pl.pallas_call(whole_kernel, in_specs=[vmem] * 6 + [smem] * 3, out_specs=...  64.9 us
    unnamed x1, local copies, waits for them, and re-layouts  1.67 us

profile of v2, /device:TPU:13, one launch (start us, length us, event | category | flops | bytes accessed | tf_op | source)
XLA Modules:
  0.0 66.6 jit_solution(16828344261752862414)
XLA Ops:
  0.0 64.9 %whole.1 = f32[16,4096]{1,0:T(8,128)} custom-call(f32[32,4096]{1,0:T(8,128)} %bitcast.6, f32[16,4096]{1,0:T(8,128)} %bitcast.7, f32[8,128,512]{2,1,0:T(8,128)} %interp.1, f32[1,128,1024]{2,1,0:T(8,128)} %basis.1, s32[8,128]{1,0:T(8,128)} %leaf_skel.1, s32[1,128]{1,0:T(1,128)} %node_skel.1, s32[4,8]{1,0:T(4,128)} %bitcast.9, s32[8,16]{1,0:T(8,128)} %bitcast.8, ...), custom_call_target="tpu_custom_call" | custom-call | flops 25769803776 | bytes 8388608 | tf_op jit(solution)/shard_map/whole/pallas_call | solution.py:268
  64.9 1.7 %copy.11 = f32[4096,16]{0,1:T(8,128)} copy(f32[4096,16]{0,1:T(8,128)} %bitcast.5) | data formatting | bytes 524288

commit v3 on v2

--- a/solution.py
+++ b/solution.py
@@ -135,14 +135,6 @@
         )
 
     to_up, to_down = near_copy(up, 0, 0), near_copy(down, 2 * leaves, 1)
-
-    @pl.when(flat < devices - 1)
-    def _():
-        to_up.start()
-
-    @pl.when(flat > 0)
-    def _():
-        to_down.start()
 
     def block_copy(position, core, to, send):
         slot = leaf_at(position) * 2 + core
@@ -185,16 +177,6 @@
 
     lax.fori_loop(0, leaves, own_tile, 0)
 
-    @pl.when(flat < devices - 1)
-    def _():
-        to_up.wait_send()
-        to_down.wait_recv()
-
-    @pl.when(flat > 0)
-    def _():
-        to_down.wait_send()
-        to_up.wait_recv()
-
     def ring_step(s, carry):
         block_copy(here - 1 - s, sub, right, right_send.at[s]).wait_recv()
 
@@ -215,6 +197,52 @@
             to_pair(here + 1 + s).start()
 
         return carry
+
+    early = min(3, half)
+    lax.fori_loop(0, early, ring_step, 0)
+
+    @pl.when(flat < devices - 1)
+    def _():
+        to_up.start()
+
+    @pl.when(flat > 0)
+    def _():
+        to_down.start()
+
+    lax.fori_loop(early, half, ring_step, 0)
+
+    def finish(q, carry):
+        block_copy(q, 1 - sub, pair, pair_send.at[q]).wait_recv()
+        block_copy(q, sub, pair, pair_send.at[q]).wait_send()
+        return carry
+
+    lax.fori_loop(0, ring, finish, 0)
+    for s in range(half):
+        to_right(s).wait_send()
+    for s in range(other):
+        to_left(s).wait_send()
+
+    def far_tiles(l, carry):
+        a = a_all[l]
+        total = acc[l]
+        per_tile = size // skel
+        for f in range(0, far_node.shape[1], per_tile):
+            group = [table[far_owner[l, i], far_node[l, i]] for i in range(f, f + per_tile)]
+            total = total + tile(a, jnp.concatenate(group, 1), dims)
+        acc[l] = total
+        return carry
+
+    lax.fori_loop(0, leaves, far_tiles, 0)
+
+    @pl.when(flat < devices - 1)
+    def _():
+        to_up.wait_send()
+        to_down.wait_recv()
+
+    @pl.when(flat > 0)
+    def _():
+        to_down.wait_send()
+        to_up.wait_recv()
 
     def near_tiles(l, carry):
         a = a_all[l]
@@ -223,34 +251,11 @@
             place = near_list[n, l] - (flat - 1) * leaves
             block = near[jnp.clip(place, 0, 3 * leaves - 1)]
             total = total + tile(a, block, dims)
-        acc[l] = total
-        return lax.fori_loop(l * half // leaves, (l + 1) * half // leaves, ring_step, carry)
-
-    lax.fori_loop(0, leaves, near_tiles, 0)
-
-    def finish(q, carry):
-        block_copy(q, 1 - sub, pair, pair_send.at[q]).wait_recv()
-        block_copy(q, sub, pair, pair_send.at[q]).wait_send()
-        return carry
-
-    lax.fori_loop(0, ring, finish, 0)
-    for s in range(half):
-        to_right(s).wait_send()
-    for s in range(other):
-        to_left(s).wait_send()
-
-    def far_tiles(l, carry):
-        a = a_all[l]
-        total = acc[l]
-        per_tile = size // skel
-        for f in range(0, far_node.shape[1], per_tile):
-            group = [table[far_owner[l, i], far_node[l, i]] for i in range(f, f + per_tile)]
-            total = total + tile(a, jnp.concatenate(group, 1), dims)
         cut = pl.ds(pl.multiple_of(l * size, size), size)
         out[:, cut] = total[:columns] + total[columns:]
         return carry
 
-    lax.fori_loop(0, leaves, far_tiles, 0)
+    lax.fori_loop(0, leaves, near_tiles, 0)
 
 
 def per_device(

time: 66.7 us -> 61.6 us (0.924)
  Pallas kernels: 64.9 us -> 59.2 us
    pallas_call x1, Pallas kernels: 64.9 us -> 59.2 us  [per_device(): pl.pallas_call(whole_kernel, in_specs=[vmem] * 6 + [smem] * 3, out_specs=...]
where the time goes in v3:
time: 61.6 us; the launch traced here: 60.9 us
  Pallas kernels  59.2 us (96%)
  local copies, waits for them, and re-layouts  1.67 us (3%)
    pallas_call x1, Pallas kernels, per_device(): pl.pallas_call(whole_kernel, in_specs=[vmem] * 6 + [smem] * 3, out_specs=...  59.2 us
    unnamed x1, local copies, waits for them, and re-layouts  1.67 us

profile of v3, /device:TPU:13, one launch (start us, length us, event | category | flops | bytes accessed | tf_op | source)
XLA Modules:
  0.0 60.9 jit_solution(2090713358626371303)
XLA Ops:
  0.0 59.2 %whole.1 = f32[16,4096]{1,0:T(8,128)} custom-call(f32[32,4096]{1,0:T(8,128)} %bitcast.6, f32[16,4096]{1,0:T(8,128)} %bitcast.7, f32[8,128,512]{2,1,0:T(8,128)} %interp.1, f32[1,128,1024]{2,1,0:T(8,128)} %basis.1, s32[8,128]{1,0:T(8,128)} %leaf_skel.1, s32[1,128]{1,0:T(1,128)} %node_skel.1, s32[4,8]{1,0:T(4,128)} %bitcast.9, s32[8,16]{1,0:T(8,128)} %bitcast.8, ...), custom_call_target="tpu_custom_call" | custom-call | flops 25769803776 | bytes 8388608 | tf_op jit(solution)/shard_map/whole/pallas_call | solution.py:273
  59.2 1.7 %copy.11 = f32[4096,16]{0,1:T(8,128)} copy(f32[4096,16]{0,1:T(8,128)} %bitcast.5) | data formatting | bytes 524288

commit v4 on v3

--- a/solution.py
+++ b/solution.py
@@ -198,7 +198,7 @@
 
         return carry
 
-    early = min(3, half)
+    early = half
     lax.fori_loop(0, early, ring_step, 0)
 
     @pl.when(flat < devices - 1)

time: 61.6 us -> 61.6 us (level)
  no operation moved by 1% of the time
where the time goes in v4:
time: 61.6 us; the launch traced here: 60.9 us
  Pallas kernels  59.2 us (96%)
  local copies, waits for them, and re-layouts  1.67 us (3%)
    pallas_call x1, Pallas kernels, per_device(): pl.pallas_call(whole_kernel, in_specs=[vmem] * 6 + [smem] * 3, out_specs=...  59.2 us
    unnamed x1, local copies, waits for them, and re-layouts  1.67 us

profile of v4, /device:TPU:13, one launch (start us, length us, event | category | flops | bytes accessed | tf_op | source)
XLA Modules:
  0.0 60.9 jit_solution(16428727190490058758)
XLA Ops:
  0.0 59.2 %whole.1 = f32[16,4096]{1,0:T(8,128)} custom-call(f32[32,4096]{1,0:T(8,128)} %bitcast.6, f32[16,4096]{1,0:T(8,128)} %bitcast.7, f32[8,128,512]{2,1,0:T(8,128)} %interp.1, f32[1,128,1024]{2,1,0:T(8,128)} %basis.1, s32[8,128]{1,0:T(8,128)} %leaf_skel.1, s32[1,128]{1,0:T(1,128)} %node_skel.1, s32[4,8]{1,0:T(4,128)} %bitcast.9, s32[8,16]{1,0:T(8,128)} %bitcast.8, ...), custom_call_target="tpu_custom_call" | custom-call | flops 25769803776 | bytes 8388608 | tf_op jit(solution)/shard_map/whole/pallas_call | solution.py:273
  59.2 1.7 %copy.11 = f32[4096,16]{0,1:T(8,128)} copy(f32[4096,16]{0,1:T(8,128)} %bitcast.5) | data formatting | bytes 524288
